TPU v7x, 256 devices: a whole 4x4x8 slice. The times are simulated.
256 devices in a mesh: row: 8 (over x, y_hi), col: 32 (over y_lo, z, core).
Axes of the slice: x: 4, y: 4 (y_hi: 2, y_lo: 2; y = y_hi * 2 + y_lo), z: 8, core: 2. Of those that a mesh axis runs over, the one named last changes fastest.
Arguments:
- x_blocks: float32 [8, 128, 128, 128], P('row', 'col'), may hold values from -0.5 to 0.5
- x_rows: int32 [8, 128], P('row', 'col'), may hold values from 0 to 75, as said below
- x_cols: int32 [8, 128], P('row', 'col'), may hold values from 0 to 18, as said below
- y_blocks: float32 [608, 32, 128, 128], P('row', 'col'), may hold values from -6 to 6
- y_cols: int32 [608, 32], P('row', 'col'), may hold values from 0 to 18, as said below
- z_rows: int32 [8, 1280], P('row', 'col'), may hold values from 0 to 75, as said below
- z_cols: int32 [8, 1280], P('row', 'col'), may hold values from 0 to 18, as said below
Outputs:
- z_blocks: float32 [8, 1280, 128, 128], P('row', 'col')
Inputs may be any that keep to these rules, and one draw needn't show every extreme that they name: `x_rows`: position of a stored block of X inside its grid cell of 76 block rows; positions may repeat. `x_cols`: position of a stored block of X inside its grid cell of 19 block columns. `y_cols`: position of a stored block of Y inside its column cell of 19 block columns. `z_rows`: every retained position of the product receives at least one product of a stored block of X with a stored block of Y; positions may repeat. `z_cols`: column position of a retained product block inside its cell.
All inputs are finite; a program needn't handle non-finite values.
Results may differ from a plain program's by a relative error of at most 0.0003.
Values sent between devices are 32-bit elements; how exact they have to be, the bound alone decides.
No kernel may reach another device: no remote copies, remote signals or barrier semaphores. Data moves between devices by JAX's collectives and lax.ppermute only.
A program may use at most 128 MiB of HBM per device.

v0:
```python
import functools

import jax
import jax.numpy as jnp
from jax import lax
from jax.experimental import pallas as pl
from jax.experimental.pallas import tpu as pltpu
from jax.sharding import Mesh
from jax.sharding import PartitionSpec as P

LANES = 128
SLOTS = (5, 6, 7, 8, 9, 10, 11, 12, 14, 16)
TOGETHER = 8
HBM = pl.BlockSpec(memory_space=pltpu.HBM)
ANY = pl.BlockSpec(memory_space=pl.ANY)
SMEM = pl.BlockSpec(memory_space=pltpu.SMEM)
VMEM = pl.BlockSpec(memory_space=pltpu.VMEM)


X_PLACE, OWNER, SLOT, TARGET, INNER, TOTAL, FIRST = range(7)
ME, PICK = 126, 127


def sheet_kernel(panel, rest, sheet, *, per_cell):
    cols = panel.shape[0]
    got = panel[...].astype(jnp.float32)
    lane = lax.broadcasted_iota(jnp.int32, (LANES, LANES), 1)
    up = lax.broadcasted_iota(jnp.int32, (LANES, LANES), 0)
    cell = lax.broadcasted_iota(jnp.int32, (cols, LANES), 0)
    mine = cell == lax.broadcasted_iota(jnp.int32, (cols, LANES), 1) // per_cell
    lines = []
    for base in (0, per_cell):
        repeated = jnp.dot(
            got,
            (up == base + lane % per_cell).astype(jnp.float32),
            preferred_element_type=jnp.float32,
        )
        lines.append(jnp.sum(jnp.where(mine, repeated, 0.0), axis=0, keepdims=True))
    whole = jnp.concatenate([v.astype(jnp.int32) for v in lines] + [rest[...]], axis=0)
    for r in range(sheet.shape[0]):
        sheet[r] = whole


def plan_kernel(
    info, plan, pick, spread, *, rows, cell_width, per_cell, group, half, targets, panel_rows
):
    shape = (rows, LANES)
    lane = lax.broadcasted_iota(jnp.int32, shape, 1)
    row = lax.broadcasted_iota(jnp.int32, shape, 0)
    x_row, x_col = info[:, 0, :], info[:, 1, :]
    z_code = info[:, 2, :] * cell_width + info[:, 3, :]
    y_col = info[:, 4, :].astype(jnp.float32)
    owner = lane // group
    inner = (lane // per_cell) % (group // per_cell) * cell_width + x_col
    spread[...] = lax.dot_general(
        y_col,
        (row == owner).astype(jnp.float32),
        (((0,), (0,)), ((), ())),
        preferred_element_type=jnp.float32,
    )
    met = jnp.zeros(shape, jnp.float32)
    for k in range(panel_rows):
        met = jnp.where(inner == k, spread[k : k + 1, :], met)
    code = x_row * cell_width + met.astype(jnp.int32)
    target = jnp.full(shape, -1, jnp.int32)
    first = lane
    for s in reversed(range(targets)):
        wanted = z_code[:, s : s + 1]
        target = jnp.where(code == wanted, s, target)
        first = jnp.where(z_code == wanted, s, first)
    used = target >= 0
    key = jnp.where(used, inner, -1 - lane)
    place = lane % group
    repeat = jnp.zeros(shape, jnp.int32)
    for d in range(1, group):
        same = (pltpu.roll(key, d, 1) == key) & (place >= d)
        repeat = jnp.where(same, d, repeat)
    sent = used & (repeat == 0)
    sent_f = sent.astype(jnp.float32)
    up = lax.broadcasted_iota(jnp.int32, (LANES, LANES), 0)
    across = lax.broadcasted_iota(jnp.int32, (LANES, LANES), 1)
    together = (up // group) == (across // group)
    before = (together & (up < across)).astype(jnp.float32)
    slot = jnp.dot(sent_f, before, preferred_element_type=jnp.float32).astype(jnp.int32)
    count = jnp.dot(sent_f, together.astype(jnp.float32), preferred_element_type=jnp.float32)
    held = slot
    for d in range(1, group):
        held = jnp.where(repeat == d, pltpu.roll(slot, d, 1), held)
    me = lax.axis_index("x") * lax.axis_size("y_hi") + lax.axis_index("y_hi")
    side = lax.axis_index("y_lo")

    own_first = (LANES - group * me) % LANES
    mine = lambda v: pltpu.roll(v, own_first, 1)
    sent_slot, sent_row = mine(jnp.where(sent, slot, -1)), mine(inner)
    blocks = jnp.zeros(shape, jnp.int32)
    for t in range(group):
        blocks = jnp.where(lane == sent_slot[:, t : t + 1], sent_row[:, t : t + 1], blocks)
    plan[0] = blocks
    plan[1] = jnp.where(lane == ME, me, mine(count.astype(jnp.int32)))

    def own(v):
        return jnp.sum(jnp.where(row == me, v.astype(jnp.float32), 0.0), axis=0, keepdims=True)

    used_f = used.astype(jnp.float32)
    rank = jnp.dot(used_f, (up < across).astype(jnp.float32), preferred_element_type=jnp.float32)
    chosen = (own(rank).astype(jnp.int32) == up) & (own(used_f) > 0.0)
    p = lane[:1]
    cell = p // per_cell
    facts = jnp.concatenate(
        [
            (
                cell % half * (2 * per_cell)
                + jnp.where(cell // half == side, 0, per_cell)
                + p % per_cell
            ).astype(jnp.float32),
            owner[:1].astype(jnp.float32),
            own(held),
            own(target),
            own(inner),
            jnp.zeros((3, LANES), jnp.float32),
        ]
    )
    listed = lax.dot_general(
        facts,
        chosen.astype(jnp.float32),
        (((1,), (1,)), ((), ())),
        preferred_element_type=jnp.float32,
    )
    total = jnp.sum(own(used_f), axis=1, keepdims=True)
    most = jnp.max(jnp.where(owner == row, 0.0, count)).astype(jnp.int32)
    choice = jnp.int32(0)
    for limit in SLOTS[:-1]:
        choice = choice + (most > limit).astype(jnp.int32)
    pick[0] = choice
    scalars = jnp.where(
        lane == ME, me.astype(jnp.float32), jnp.where(lane == PICK, choice.astype(jnp.float32), total)
    )
    plan[2] = jnp.where(
        row == TOTAL, scalars, jnp.where(row == FIRST, own(first), listed)
    ).astype(jnp.int32)


def pack_kernel(plan, y_blocks, out, sem, *, rows):
    me = plan[1, 0, ME]
    started = jnp.int32(0)
    for r in range(rows):
        count = jnp.where(me == r, 0, plan[1, r, 0])

        @pl.loop(0, count)
        def _(j):
            pltpu.make_async_copy(y_blocks.at[plan[0, r, j]], out.at[r, j], sem).start()

        started = started + count

    @pl.loop(0, started)
    def _(_):
        pltpu.make_async_copy(y_blocks.at[0], out.at[0, 0], sem).wait()


def nothing_kernel(*out):
    pass


def product_kernel(plan, x_all, y_blocks, *refs, targets):
    got, (out, x_held, y_held, sums, into, in_sem, out_sem) = refs[:-7], refs[-7:]
    me, pick, total = plan[2, TOTAL, ME], plan[2, TOTAL, PICK], plan[2, TOTAL, 0]

    for i, brought in enumerate(got):

        @pl.when(pick == i)
        def _():
            @pl.loop(0, total)
            def _(n):
                place, owner = plan[2, X_PLACE, n], plan[2, OWNER, n]
                here = owner == me
                sem = in_sem.at[n // TOGETHER]
                pltpu.make_async_copy(x_all.at[place], x_held.at[n], sem).start()

                @pl.when(here)
                def _():
                    pltpu.make_async_copy(
                        y_blocks.at[plan[2, INNER, n]], y_held.at[n], sem
                    ).start()

                @pl.when(jnp.logical_not(here))
                def _():
                    pltpu.make_async_copy(
                        brought.at[owner, plan[2, SLOT, n]], y_held.at[n], sem
                    ).start()

                into[n] = plan[2, TARGET, n]

    for j in range(TOGETHER - 1):
        into[total + j] = targets
    sums[...] = jnp.zeros_like(sums)
    dot = functools.partial(jnp.dot, preferred_element_type=jnp.float32)

    @pl.loop(0, (total + TOGETHER - 1) // TOGETHER)
    def _(i):
        n = i * TOGETHER
        for j in range(TOGETHER):

            @pl.when(n + j < total)
            def _():
                pltpu.make_async_copy(x_all.at[0], x_held.at[n + j], in_sem.at[i]).wait()
                pltpu.make_async_copy(y_blocks.at[0], y_held.at[n + j], in_sem.at[i]).wait()

        products = []
        for j in range(TOGETHER):
            x, y = x_held[n + j], y_held[n + j]
            x_hi, y_hi = x.astype(jnp.bfloat16), y.astype(jnp.bfloat16)
            x_lo = (x - x_hi.astype(jnp.float32)).astype(jnp.bfloat16)
            y_lo = (y - y_hi.astype(jnp.float32)).astype(jnp.bfloat16)
            products.append(
                dot(
                    jnp.concatenate([x_hi, x_lo, x_hi], axis=1),
                    jnp.concatenate([y_hi, y_hi, y_lo], axis=0),
                )
            )
        for j in range(TOGETHER):
            sums[into[n + j]] += products[j]

    for s in range(targets):
        pltpu.make_async_copy(sums.at[plan[2, FIRST, s]], out.at[s], out_sem).start()
    for s in range(targets):
        pltpu.make_async_copy(sums.at[0], out.at[s], out_sem).wait()


def local(x_blocks, x_rows, x_cols, y_blocks, y_cols, z_rows, z_cols):
    row_axes, col_axes = ("x", "y_hi"), ("y_lo", "z", "core")
    rows, cols = lax.axis_size(row_axes), lax.axis_size(col_axes)
    x_blocks = x_blocks[0]
    y_blocks = y_blocks[:, 0]
    per_cell, edge = x_blocks.shape[0], x_blocks.shape[-1]
    panel_rows = y_blocks.shape[0]
    targets = z_rows.shape[1]
    group = cols * per_cell // rows
    cell_width = panel_rows * rows // cols
    half = cols // 2
    block = (edge, edge)

    own = jnp.pad(jnp.concatenate([x_rows[0], x_cols[0]]), (0, LANES - 2 * per_cell))
    own = jnp.broadcast_to(own, (cols, 1, LANES))
    rest = jnp.stack(
        [jnp.pad(v, (0, LANES - v.shape[0])) for v in (z_rows[0], z_cols[0], y_cols[:, 0])]
    )
    own, x_blocks = lax.optimization_barrier((own, x_blocks))
    panel = lax.all_to_all(own, col_axes, 0, 0, tiled=True).reshape(cols, LANES)

    across = lax.ppermute(x_blocks, "y_lo", [(0, 1), (1, 0)])
    pair = jnp.concatenate([x_blocks, across], axis=0)
    panel, rest, pair = lax.optimization_barrier((panel, rest, pair))
    x_all = lax.all_gather(pair, ("z", "core"), axis=0, tiled=True)

    sheet = pl.pallas_call(
        functools.partial(sheet_kernel, per_cell=per_cell),
        out_shape=jax.ShapeDtypeStruct((rows, 5, LANES), jnp.int32),
        in_specs=[VMEM] * 2,
        out_specs=VMEM,
        compiler_params=pltpu.CompilerParams(vmem_limit_bytes=4 * 2**20),
        name="sheet",
    )(panel, rest)
    info = lax.all_to_all(sheet, row_axes, 0, 0, tiled=True)

    plan, pick = pl.pallas_call(
        functools.partial(
            plan_kernel,
            rows=rows,
            cell_width=cell_width,
            per_cell=per_cell,
            group=group,
            half=half,
            targets=targets,
            panel_rows=panel_rows,
        ),
        out_shape=(
            jax.ShapeDtypeStruct((3, rows, LANES), jnp.int32),
            jax.ShapeDtypeStruct((1,), jnp.int32),
        ),
        in_specs=[VMEM],
        out_specs=(VMEM, SMEM),
        scratch_shapes=[pltpu.VMEM((LANES, LANES), jnp.float32)],
        compiler_params=pltpu.CompilerParams(vmem_limit_bytes=4 * 2**20),
        name="plan",
    )(info)

    def room(slots):
        return jax.ShapeDtypeStruct((rows, slots) + block, jnp.float32)

    def with_slots(slots):
        def branch(plan, y_blocks):
            packed = pl.pallas_call(
                functools.partial(pack_kernel, rows=rows),
                out_shape=room(slots),
                in_specs=[SMEM, HBM],
                out_specs=VMEM,
                scratch_shapes=[pltpu.SemaphoreType.DMA],
                compiler_params=pltpu.CompilerParams(vmem_limit_bytes=40 * 2**20),
                name="pack",
            )(plan, y_blocks)
            others = [s for s in SLOTS if s != slots]
            unused = pl.pallas_call(
                nothing_kernel,
                out_shape=[room(s) for s in others],
                out_specs=[HBM] * len(others),
                name="unused",
            )()
            packed, unused = lax.optimization_barrier((packed, unused))
            unused = dict(zip(others, unused, strict=True))
            got = lax.all_to_all(packed, row_axes, 0, 0, tiled=True)
            return [got if s == slots else unused[s] for s in SLOTS]

        return branch

    got = lax.switch(pick[0], [with_slots(s) for s in SLOTS], plan, y_blocks)

    out = pl.pallas_call(
        functools.partial(product_kernel, targets=targets),
        out_shape=jax.ShapeDtypeStruct((targets,) + block, jnp.float32),
        in_specs=[SMEM] + [HBM] * (2 + len(SLOTS)),
        out_specs=HBM,
        scratch_shapes=[
            pltpu.VMEM((LANES,) + block, jnp.float32),
            pltpu.VMEM((LANES,) + block, jnp.float32),
            pltpu.VMEM((targets + 1,) + block, jnp.float32),
            pltpu.SMEM((LANES + TOGETHER,), jnp.int32),
            pltpu.SemaphoreType.DMA((LANES // TOGETHER,)),
            pltpu.SemaphoreType.DMA,
        ],
        compiler_params=pltpu.CompilerParams(vmem_limit_bytes=60 * 2**20),
        name="products",
    )(plan, x_all, y_blocks, *got)
    return out[None]


def solution(mesh):
    chips = Mesh(mesh.devices.reshape(4, 2, 2, 8, 2), ("x", "y_hi", "y_lo", "z", "core"))
    row, col = ("x", "y_hi"), ("y_lo", "z", "core")
    flat, blocks = P(row, col), P(row, col, None, None)
    return jax.shard_map(
        local,
        mesh=chips,
        in_specs=(blocks, flat, flat, blocks, flat, flat, flat),
        out_specs=blocks,
        check_vma=False,
    )
```

profile of v0, /device:TPU:2, one launch (start us, length us, event | category | flops | bytes accessed | tf_op | source)
XLA Modules:
  0.0 115.8 jit_solution(7905497996742826857)
XLA Ops:
  6.5 0.7 pad_add_fusion.1
  7.3 0.6 broadcast_in_dim.6
  7.9 1.6 %collective-permute-start = (f32[4,128,128]{2,1,0:T(8,128)}, f32[4,128,128]{2,1,0:T(8,128)S(1)}, u32[]{:S(2)}, u32[]{:S(2)}) collective-permute-start(f32[4,128,128]{2,1,0:T(8,128)} %bitcast.28), channel_id=1, source_target_pairs={{0,16},{16,0},{1,17},{17,1},{2,18},{18,2},{3,19},{19,3},{4,20},{20... | collective-permute-start | bytes 786440 | tf_op jit(solution)/shard_map/ppermute | solution.py:250
  9.5 8.9 %all-to-all-start.10 = ((s32[32,1,128]{2,1,0:T(1,128)}), s32[32,1,128]{2,1,0:T(1,128)S(1)}, u32[]{:S(2)}, u32[]{:S(2)}) async-start(s32[32,1,128]{2,1,0:T(1,128)} %broadcast_in_dim.6), calls=%async_computation.10 | async-start | bytes 32768 | tf_op jit(solution)/shard_map/all_to_all | solution.py:248
  18.3 0.0 all-gather.2.cloned.1.call-start
  18.4 0.7 pad_bitcast_fusion.2
  19.0 0.7 pad_bitcast_fusion
  19.7 0.0 collective-permute-done
  19.7 1.8 %pad_maximum_fusion = f32[8,128,128]{2,1,0:T(8,128)} fusion(f32[4,128,128]{2,1,0:T(8,128)S(1)} %collective-permute-done, f32[4,128,128]{2,1,0:T(8,128)} %bitcast.29), kind=kLoop, calls=%fused_computation | loop fusion | flops 131072 | bytes 1048576 | tf_op jit(solution)/shard_map/concatenate | solution.py:251
  21.5 5.2 %all-to-all-done.10 = s32[32,1,128]{2,1,0:T(1,128)S(1)} async-done(((s32[32,1,128]{2,1,0:T(1,128)}), s32[32,1,128]{2,1,0:T(1,128)S(1)}, u32[]{:S(2)}, u32[]{:S(2)}) %all-to-all-start.10) | async-done | bytes 16416 | tf_op jit(solution)/shard_map/all_to_all | solution.py:248
  26.7 0.0 all-gather.2.cloned.1.call-update
  26.8 0.1 sheet.1
  26.9 13.4 %all_to_all.60.info = s32[8,5,128]{2,1,0:T(8,128)S(1)} all-to-all(s32[8,5,128]{2,1,0:T(8,128)S(1)} %sheet.1), channel_id=1, replica_groups=mesh['x'=4,'y_hi'=2,'y_lo'=2,'z'=8,'core'=2] {'x','y_hi'}, dimensions={0} | all-to-all | bytes 40960 | tf_op jit(solution)/shard_map/all_to_all | solution.py:263
  40.3 1.5 %plan.1 = (s32[3,8,128]{2,1,0:T(8,128)S(1)}, s32[1]{0:T(128)}) custom-call(s32[8,5,128]{2,1,0:T(8,128)S(1)} %all_to_all.60.info), custom_call_target="tpu_custom_call" | custom-call | tf_op jit(solution)/shard_map/plan/pallas_call | solution.py:265
  42.4 61.0 %conditional.1 = (f32[8,5,128,128]{3,2,1,0:T(8,128)S(1)}, f32[8,6,128,128]{3,2,1,0:T(8,128)}, f32[8,7,128,128]{3,2,1,0:T(8,128)}, f32[8,8,128,128]{3,2,1,0:T(8,1...) conditional(s32[]{:T(128)} %bitcast.11, ...), branch_computations={%region_0.1_spmd, %region_1.2_spmd, %region_2.3_spmd, %region_3.4_... | conditional | bytes 16777296 | solution.py:315
  42.5 2.3 %pack.14 = f32[8,9,128,128]{3,2,1,0:T(8,128)S(1)} custom-call(s32[3,8,128]{2,1,0:T(8,128)S(1)} %get-tuple-element.129.plan, f32[76,128,128]{2,1,0:T(8,128)} %get-tuple-element.130.y_blocks), custom_call_target="tpu_custom_call" | custom-call | tf_op jit(solution)/shard_map/cond/branch_4_fun/pack/pallas_call | solution.py:292
  44.8 58.6 %all_to_all.54 = f32[8,9,128,128]{3,2,1,0:T(8,128)} all-to-all(f32[8,9,128,128]{3,2,1,0:T(8,128)S(1)} %pack.14), channel_id=1, replica_groups=mesh['x'=4,'y_hi'=2,'y_lo'=2,'z'=8,'core'=2] {'x','y_hi'}, dimensions={0} | all-to-all | bytes 9437184 | tf_op jit(solution)/shard_map/cond/branch_4_fun/all_to_all | solution.py:310
  103.4 0.0 all-gather.2.cloned.1.call-done.x_all
  103.4 5.5 %products.1 = f32[40,128,128]{2,1,0:T(8,128)} custom-call(s32[3,8,128]{2,1,0:T(8,128)S(1)} %get-tuple-element.276.plan, f32[128,128,128]{2,1,0:T(8,128)} %all-gather.2.cloned.1.call-done.x_all, f32[76,128,128]{2,1,0:T(8,128)} %bitcast.27, f32[8,5,128,128]{3,2,1,0:T(8,128)S(1)} %get-tuple-element.279.refs_0_, f32[8,6,128,128]{3,2,1,0:T(8,128)} %get-tuple-element.280.refs_1_, ...), custom_call_target="tpu_custom_call" | custom-call | tf_op jit(solution)/shard_map/products/pallas_call | solution.py:317
  (3 shorter events, 0.0 us)
Async XLA Ops:
  7.9 11.8 %collective-permute-start = (f32[4,128,128]{2,1,0:T(8,128)}, f32[4,128,128]{2,1,0:T(8,128)S(1)}, u32[]{:S(2)}, u32[]{:S(2)}) collective-permute-start(f32[4,128,128]{2,1,0:T(8,128)} %bitcast.28), channel_id=1, source_target_pairs={{0,16},{16,0},{1,17},{17,1},{2,18},{18,2},{3,19},{19,3},{4,20},{20... | collective-permute-start | bytes 786440 | tf_op jit(solution)/shard_map/ppermute | solution.py:250
  9.5 17.3 %all-to-all-start.10 = ((s32[32,1,128]{2,1,0:T(1,128)}), s32[32,1,128]{2,1,0:T(1,128)S(1)}, u32[]{:S(2)}, u32[]{:S(2)}) async-start(s32[32,1,128]{2,1,0:T(1,128)} %broadcast_in_dim.6), calls=%async_computation.10 | async-start | bytes 32768 | tf_op jit(solution)/shard_map/all_to_all | solution.py:248
  18.3 85.1 %all-gather.2.cloned.1.call-start = ((), (), s32[]{:S(2)}) async-start(), calls=%async_computation.12 | async-start | bytes 8912896 | tf_op jit(solution)/shard_map/all_gather | solution.py:253
Sparse Core Ops, SparseCore 0:
  26.9 52.1 all-gather.1
where the time goes:
time: 114 us; the launch traced here: 116 us
  blocking collectives  72 us (63%)
  between operations  14.1 us (12%)
  starting transfers between devices  10.5 us (9%)
  Pallas kernels  9.47 us (8%)
  waiting for transfers between devices  5.23 us (5%)
  other arithmetic  2.54 us (2%)
  local copies, waits for them, and re-layouts  1.95 us (2%)
    all_to_all x1, blocking collectives, branch(): got = lax.all_to_all(packed, row_axes, 0, 0, tiled=True)  58.6 us
    all_to_all x1, blocking collectives, local(): info = lax.all_to_all(sheet, row_axes, 0, 0, tiled=True)  13.4 us
    all_to_all x1, starting transfers between devices, local(): panel = lax.all_to_all(own, col_axes, 0, 0, tiled=True).reshape(cols, LANES)  8.85 us
    pallas_call x1, Pallas kernels, local(): pl.pallas_call(functools.partial(product_kernel, targets=targets), out_sh...  5.53 us
    all_to_all x1, waiting for transfers between devices, local(): panel = lax.all_to_all(own, col_axes, 0, 0, tiled=True).reshape(cols, LANES)  5.21 us
    pallas_call x1, Pallas kernels, branch(): pl.pallas_call(functools.partial(pack_kernel, rows=rows), out_shape=room(...  2.34 us
  transfers between devices with their start and end apart: 3, of which 1 were waited for; matrix products, arithmetic and copies ran while one was open for 3% of the time, Pallas kernels for 3%

commit v1 on v0

--- a/solution.py
+++ b/solution.py
@@ -18,7 +18,8 @@
 
 
 X_PLACE, OWNER, SLOT, TARGET, INNER, TOTAL, FIRST = range(7)
-ME, PICK = 126, 127
+ME, PICK, BASE = 126, 127, 125
+BASES, EXTRA = (8, 9, 10), 2
 
 
 def sheet_kernel(panel, rest, sheet, *, per_cell):
@@ -127,24 +128,36 @@
         preferred_element_type=jnp.float32,
     )
     total = jnp.sum(own(used_f), axis=1, keepdims=True)
-    most = jnp.max(jnp.where(owner == row, 0.0, count)).astype(jnp.int32)
-    choice = jnp.int32(0)
+    needed = jnp.where(owner == row, 0, count.astype(jnp.int32))
+    most = jnp.max(needed)
+    slots = jnp.int32(0)
     for limit in SLOTS[:-1]:
-        choice = choice + (most > limit).astype(jnp.int32)
+        slots = slots + (most > limit).astype(jnp.int32)
+    base, choice = jnp.int32(SLOTS[-1]), slots
+    apart = (row - owner + rows) % rows
+    for i, few in reversed(list(enumerate(BASES))):
+        over = needed > few
+        nearest = jnp.min(jnp.where(over, apart, rows))
+        only = jnp.max(jnp.where(over, apart, 0)) == nearest
+        fits = only & (most <= few + EXTRA)
+        slots = jnp.where(fits, SLOTS.index(few), slots)
+        base = jnp.where(fits, few, base)
+        choice = jnp.where(fits, len(SLOTS) + (rows - 1) * i + nearest - 1, choice)
     pick[0] = choice
-    scalars = jnp.where(
-        lane == ME, me.astype(jnp.float32), jnp.where(lane == PICK, choice.astype(jnp.float32), total)
-    )
+    scalars = total.astype(jnp.int32)
+    for at, v in ((ME, me), (PICK, slots), (BASE, base)):
+        scalars = jnp.where(lane == at, v, scalars)
+    scalars = scalars.astype(jnp.float32)
     plan[2] = jnp.where(
         row == TOTAL, scalars, jnp.where(row == FIRST, own(first), listed)
     ).astype(jnp.int32)
 
 
 def pack_kernel(plan, y_blocks, out, sem, *, rows):
-    me = plan[1, 0, ME]
+    me, slots = plan[1, 0, ME], out.shape[1]
     started = jnp.int32(0)
     for r in range(rows):
-        count = jnp.where(me == r, 0, plan[1, r, 0])
+        count = jnp.where(me == r, 0, jnp.minimum(plan[1, r, 0], slots))
 
         @pl.loop(0, count)
         def _(j):
@@ -157,12 +170,26 @@
         pltpu.make_async_copy(y_blocks.at[0], out.at[0, 0], sem).wait()
 
 
+def pack_extra_kernel(plan, y_blocks, out, sem, *, rows, slots, apart):
+    r = (plan[1, 0, ME] + apart) % rows
+    count = jnp.clip(plan[1, r, 0] - slots, 0, EXTRA)
+
+    @pl.loop(0, count)
+    def _(j):
+        pltpu.make_async_copy(y_blocks.at[plan[0, r, slots + j]], out.at[j], sem).start()
+
+    @pl.loop(0, count)
+    def _(j):
+        pltpu.make_async_copy(y_blocks.at[0], out.at[j], sem).wait()
+
+
 def nothing_kernel(*out):
     pass
 
 
-def product_kernel(plan, x_all, y_blocks, *refs, targets):
+def product_kernel(plan, x_all, y_blocks, extra, *refs, targets):
     got, (out, x_held, y_held, sums, into, in_sem, out_sem) = refs[:-7], refs[-7:]
+    base = plan[2, TOTAL, BASE]
     me, pick, total = plan[2, TOTAL, ME], plan[2, TOTAL, PICK], plan[2, TOTAL, 0]
 
     for i, brought in enumerate(got):
@@ -182,11 +209,15 @@
                         y_blocks.at[plan[2, INNER, n]], y_held.at[n], sem
                     ).start()
 
-                @pl.when(jnp.logical_not(here))
+                slot = plan[2, SLOT, n]
+
+                @pl.when(jnp.logical_not(here) & (slot < base))
                 def _():
-                    pltpu.make_async_copy(
-                        brought.at[owner, plan[2, SLOT, n]], y_held.at[n], sem
-                    ).start()
+                    pltpu.make_async_copy(brought.at[owner, slot], y_held.at[n], sem).start()
+
+                @pl.when(jnp.logical_not(here) & (slot >= base))
+                def _():
+                    pltpu.make_async_copy(extra.at[slot - base], y_held.at[n], sem).start()
 
                 into[n] = plan[2, TARGET, n]
 
@@ -287,37 +318,59 @@
     def room(slots):
         return jax.ShapeDtypeStruct((rows, slots) + block, jnp.float32)
 
-    def with_slots(slots):
-        def branch(plan, y_blocks):
-            packed = pl.pallas_call(
-                functools.partial(pack_kernel, rows=rows),
-                out_shape=room(slots),
-                in_specs=[SMEM, HBM],
-                out_specs=VMEM,
-                scratch_shapes=[pltpu.SemaphoreType.DMA],
-                compiler_params=pltpu.CompilerParams(vmem_limit_bytes=40 * 2**20),
-                name="pack",
-            )(plan, y_blocks)
+    more = jax.ShapeDtypeStruct((EXTRA,) + block, jnp.float32)
+
+    def pack(kernel, shape, plan, y_blocks):
+        return pl.pallas_call(
+            functools.partial(kernel, rows=rows),
+            out_shape=shape,
+            in_specs=[SMEM, HBM],
+            out_specs=VMEM,
+            scratch_shapes=[pltpu.SemaphoreType.DMA],
+            compiler_params=pltpu.CompilerParams(vmem_limit_bytes=40 * 2**20),
+            name="pack",
+        )(plan, y_blocks)
+
+    def nothing(shapes):
+        return pl.pallas_call(
+            nothing_kernel, out_shape=shapes, out_specs=[HBM] * len(shapes), name="unused"
+        )()
+
+    def with_slots(slots, apart=0):
+        def exchange(plan, y_blocks):
+            packed = pack(pack_kernel, room(slots), plan, y_blocks)
+            return lax.all_to_all(packed, row_axes, 0, 0, tiled=True)
+
+        def branch(plan, chosen, y_blocks):
             others = [s for s in SLOTS if s != slots]
-            unused = pl.pallas_call(
-                nothing_kernel,
-                out_shape=[room(s) for s in others],
-                out_specs=[HBM] * len(others),
-                name="unused",
-            )()
-            packed, unused = lax.optimization_barrier((packed, unused))
-            unused = dict(zip(others, unused, strict=True))
-            got = lax.all_to_all(packed, row_axes, 0, 0, tiled=True)
-            return [got if s == slots else unused[s] for s in SLOTS]
+            unused = nothing([room(s) for s in others] + [more] * (apart == 0))
+            plan, unused = lax.optimization_barrier((plan, unused))
+            got = dict(zip(others, unused))
+            if apart:
+                kernel = functools.partial(pack_extra_kernel, slots=slots, apart=apart)
+                extra = pack(kernel, more, plan, y_blocks)
+                plan, extra = lax.optimization_barrier((plan, extra))
+                turn = [(i, (i + apart) % rows) for i in range(rows)]
+                extra = lax.ppermute(extra, row_axes, turn)
+                got[slots] = lax.cond(
+                    chosen >= 0, exchange, lambda *_: nothing([room(slots)])[0], plan, y_blocks
+                )
+            else:
+                extra = unused[-1]
+                got[slots] = exchange(plan, y_blocks)
+            return [extra] + [got[s] for s in SLOTS]
 
         return branch
 
-    got = lax.switch(pick[0], [with_slots(s) for s in SLOTS], plan, y_blocks)
+    branches = [with_slots(s) for s in SLOTS]
+    branches += [with_slots(s, apart) for s in BASES for apart in range(1, rows)]
+
+    got = lax.switch(pick[0], branches, plan, pick[0], y_blocks)
 
     out = pl.pallas_call(
         functools.partial(product_kernel, targets=targets),
         out_shape=jax.ShapeDtypeStruct((targets,) + block, jnp.float32),
-        in_specs=[SMEM] + [HBM] * (2 + len(SLOTS)),
+        in_specs=[SMEM] + [HBM] * (3 + len(SLOTS)),
         out_specs=HBM,
         scratch_shapes=[
             pltpu.VMEM((LANES,) + block, jnp.float32),

time: 114 us -> 117 us (1.026)
  the two profiles are of different devices: /device:TPU:2 before, /device:TPU:64 now
where the time goes in v1:
time: 117 us; the launch traced here: 118 us
  blocking collectives  67.4 us (58%)
  between operations  14.1 us (12%)
  starting transfers between devices  11.3 us (10%)
  Pallas kernels  10.5 us (9%)
  loops' own time  7.3 us (6%)
  waiting for transfers between devices  3.1 us (3%)
  other arithmetic  2.54 us (2%)
  local copies, waits for them, and re-layouts  1.95 us (2%)
    all_to_all x1, blocking collectives, exchange(): return lax.all_to_all(packed, row_axes, 0, 0, tiled=True)  53.1 us
    all_to_all x1, blocking collectives, local(): info = lax.all_to_all(sheet, row_axes, 0, 0, tiled=True)  14.3 us
    all_to_all x1, starting transfers between devices, local(): panel = lax.all_to_all(own, col_axes, 0, 0, tiled=True).reshape(cols, LANES)  8.27 us
    another operation x1, loops' own time, local(): got = lax.switch(pick[0], branches, plan, pick[0], y_blocks)  7.28 us
    pallas_call x1, Pallas kernels, local(): pl.pallas_call(functools.partial(product_kernel, targets=targets), out_sh...  5.52 us
    pallas_call x2, Pallas kernels, pack(): pl.pallas_call(functools.partial(kernel, rows=rows), out_shape=shape, in_...  3.22 us
    all_to_all x1, waiting for transfers between devices, local(): panel = lax.all_to_all(own, col_axes, 0, 0, tiled=True).reshape(cols, LANES)  3.06 us
  transfers between devices with their start and end apart: 4, of which 1 were waited for; matrix products, arithmetic and copies ran while one was open for 3% of the time, Pallas kernels for 4%

profile of v1, /device:TPU:64, one launch (start us, length us, event | category | flops | bytes accessed | tf_op | source)
XLA Modules:
  0.0 118.2 jit_solution(8391210939293704443)
XLA Ops:
  6.5 0.7 pad_add_fusion.1
  7.3 0.6 broadcast_in_dim.6
  7.9 1.6 %collective-permute-start.21 = (f32[4,128,128]{2,1,0:T(8,128)}, f32[4,128,128]{2,1,0:T(8,128)S(1)}, u32[]{:S(2)}, u32[]{:S(2)}) collective-permute-start(f32[4,128,128]{2,1,0:T(8,128)} %bitcast.49), channel_id=1, source_target_pairs={{0,16},{16,0},{1,17},{17,1},{2,18},{18,2},{3,19},{19,3},{4,20},{20... | collective-permute-start | bytes 786440 | tf_op jit(solution)/shard_map/ppermute | solution.py:281
  9.5 8.3 %all-to-all-start.31 = ((s32[32,1,128]{2,1,0:T(1,128)}), s32[32,1,128]{2,1,0:T(1,128)S(1)}, u32[]{:S(2)}, u32[]{:S(2)}) async-start(s32[32,1,128]{2,1,0:T(1,128)} %broadcast_in_dim.6), calls=%async_computation.31 | async-start | bytes 32768 | tf_op jit(solution)/shard_map/all_to_all | solution.py:279
  17.8 0.0 all-gather.2.cloned.1.call-start
  17.8 0.7 pad_bitcast_fusion.2
  18.5 0.7 pad_bitcast_fusion
  19.1 0.0 collective-permute-done.21
  19.2 1.8 %pad_maximum_fusion = f32[8,128,128]{2,1,0:T(8,128)} fusion(f32[4,128,128]{2,1,0:T(8,128)S(1)} %collective-permute-done.21, f32[4,128,128]{2,1,0:T(8,128)} %bitcast.50), kind=kLoop, calls=%fused_computation | loop fusion | flops 131072 | bytes 1048576 | tf_op jit(solution)/shard_map/concatenate | solution.py:282
  20.9 3.1 %all-to-all-done.31 = s32[32,1,128]{2,1,0:T(1,128)S(1)} async-done(((s32[32,1,128]{2,1,0:T(1,128)}), s32[32,1,128]{2,1,0:T(1,128)S(1)}, u32[]{:S(2)}, u32[]{:S(2)}) %all-to-all-start.31) | async-done | bytes 16416 | tf_op jit(solution)/shard_map/all_to_all | solution.py:279
  24.0 0.0 all-gather.2.cloned.1.call-update
  24.0 0.1 sheet.1
  24.2 14.3 %all_to_all.165.info = s32[8,5,128]{2,1,0:T(8,128)S(1)} all-to-all(s32[8,5,128]{2,1,0:T(8,128)S(1)} %sheet.1), channel_id=1, replica_groups=mesh['x'=4,'y_hi'=2,'y_lo'=2,'z'=8,'core'=2] {'x','y_hi'}, dimensions={0} | all-to-all | bytes 40960 | tf_op jit(solution)/shard_map/all_to_all | solution.py:294
  38.5 1.6 %plan.1 = (s32[3,8,128]{2,1,0:T(8,128)S(1)}, s32[1]{0:T(128)}) custom-call(s32[8,5,128]{2,1,0:T(8,128)S(1)} %all_to_all.165.info), custom_call_target="tpu_custom_call" | custom-call | tf_op jit(solution)/shard_map/plan/pallas_call | solution.py:296
  40.8 65.0 %conditional.22 = (f32[2,128,128]{2,1,0:T(8,128)}, f32[8,5,128,128]{3,2,1,0:T(8,128)S(1)}, f32[8,6,128,128]{3,2,1,0:T(8,128)}, f32[8,7,128,128]{3,2,1,0:T(8,128)...) conditional(s32[]{:T(128)} %clamp.3, ...), branch_computations={%region_0.1_spmd, %region_1.2_spmd, %region_2.3_spmd, %region_3.4_... | conditional | flops 2 | bytes 16777304 | solution.py:368
  40.8 0.8 pack.75
  41.6 1.4 %collective-permute-start.6 = (f32[2,128,128]{2,1,0:T(8,128)S(1)}, f32[2,128,128]{2,1,0:T(8,128)}, u32[]{:S(2)}, u32[]{:S(2)}) collective-permute-start(f32[2,128,128]{2,1,0:T(8,128)S(1)} %pack.75), channel_id=1, source_target_pairs={{0,224},{32,0},{64,32},{96,64},{128,96},{160,128},{192,160},{224,1... | collective-permute-start | bytes 393224 | tf_op jit(solution)/shard_map/cond/branch_16_fun/ppermute | solution.py:354
  43.7 55.6 %conditional.6 = (f32[8,8,128,128]{3,2,1,0:T(8,128)}) conditional(s32[]{:T(128)} %convert_element_type.48, () %tuple.203, (s32[3,8,128]{2,1,0:T(8,128)S(1)}, f32[76,128,128]{2,1,0:T(8,128)}) %tuple.204), branch_computations={%region_29.29_spmd, %region_30.30_spmd} | conditional | bytes 8388616 | solution.py:355
  43.7 2.5 %pack.74 = f32[8,8,128,128]{3,2,1,0:T(8,128)S(1)} custom-call(s32[3,8,128]{2,1,0:T(8,128)S(1)} %get-tuple-element.704.plan, f32[76,128,128]{2,1,0:T(8,128)} %get-tuple-element.705.y_blocks), custom_call_target="tpu_custom_call" | custom-call | tf_op jit(solution)/shard_map/cond/branch_16_fun/cond/branch_1_fun/pack/pallas_call | solution.py:324
  46.2 53.1 %all_to_all.150 = f32[8,8,128,128]{3,2,1,0:T(8,128)} all-to-all(f32[8,8,128,128]{3,2,1,0:T(8,128)S(1)} %pack.74), channel_id=1, replica_groups=mesh['x'=4,'y_hi'=2,'y_lo'=2,'z'=8,'core'=2] {'x','y_hi'}, dimensions={0} | all-to-all | bytes 8388608 | tf_op jit(solution)/shard_map/cond/branch_16_fun/cond/branch_1_fun/all_to_all | solution.py:342
  99.2 0.0 collective-permute-done.6
  105.8 0.0 all-gather.2.cloned.1.call-done.x_all
  105.8 5.5 %products.1 = f32[40,128,128]{2,1,0:T(8,128)} custom-call(s32[3,8,128]{2,1,0:T(8,128)S(1)} %get-tuple-element.1116.plan, f32[128,128,128]{2,1,0:T(8,128)} %all-gather.2.cloned.1.call-done.x_all, f32[76,128,128]{2,1,0:T(8,128)} %bitcast.48, f32[2,128,128]{2,1,0:T(8,128)} %get-tuple-element.1119.extra, f32[8,5,128,128]{3,2,1,0:T(8,128)S(1)} %get-tuple-element.1120.refs_0_, ...), custom_call_target="tpu_custom_call" | custom-call | tf_op jit(solution)/shard_map/products/pallas_call | solution.py:370
  (3 shorter events, 0.0 us)
Async XLA Ops:
  7.9 11.3 %collective-permute-start.21 = (f32[4,128,128]{2,1,0:T(8,128)}, f32[4,128,128]{2,1,0:T(8,128)S(1)}, u32[]{:S(2)}, u32[]{:S(2)}) collective-permute-start(f32[4,128,128]{2,1,0:T(8,128)} %bitcast.49), channel_id=1, source_target_pairs={{0,16},{16,0},{1,17},{17,1},{2,18},{18,2},{3,19},{19,3},{4,20},{20... | collective-permute-start | bytes 786440 | tf_op jit(solution)/shard_map/ppermute | solution.py:281
  9.5 14.5 %all-to-all-start.31 = ((s32[32,1,128]{2,1,0:T(1,128)}), s32[32,1,128]{2,1,0:T(1,128)S(1)}, u32[]{:S(2)}, u32[]{:S(2)}) async-start(s32[32,1,128]{2,1,0:T(1,128)} %broadcast_in_dim.6), calls=%async_computation.31 | async-start | bytes 32768 | tf_op jit(solution)/shard_map/all_to_all | solution.py:279
  17.8 88.0 %all-gather.2.cloned.1.call-start = ((), (), s32[]{:S(2)}) async-start(), calls=%async_computation.33 | async-start | bytes 8912896 | tf_op jit(solution)/shard_map/all_gather | solution.py:284
  41.6 57.6 %collective-permute-start.6 = (f32[2,128,128]{2,1,0:T(8,128)S(1)}, f32[2,128,128]{2,1,0:T(8,128)}, u32[]{:S(2)}, u32[]{:S(2)}) collective-permute-start(f32[2,128,128]{2,1,0:T(8,128)S(1)} %pack.75), channel_id=1, source_target_pairs={{0,224},{32,0},{64,32},{96,64},{128,96},{160,128},{192,160},{224,1... | collective-permute-start | bytes 393224 | tf_op jit(solution)/shard_map/cond/branch_16_fun/ppermute | solution.py:354
Sparse Core Ops, SparseCore 0:
  24.1 52.3 all-gather.1
